TPU v7x, 32 devices: a whole 2x2x4 slice. The times are simulated.
32 devices in a mesh: ch: 8 (over z, x), tok: 4 (over y, core).
Axes of the slice: x: 2, y: 2, z: 4, core: 2. Of those that a mesh axis runs over, the one named last changes fastest.
Arguments:
- inputs: bfloat16 [4, 768, 4096], P(None, 'ch', 'tok'), may hold values from -6 to 6
- out_grad: bfloat16 [4, 768, 4096], P(None, 'ch', 'tok'), may hold values from -6 to 6
- seq_lengths: int32 [4], replicated, may hold values from 2560 to 4096, as said below
- ema_alpha: float32 [768, 16], P('ch'), may hold values from -0.85 to 0.85
- ema_delta: float32 [768, 16], P('ch'), may hold values from -14 to -1.9
- ema_beta: float32 [768, 16], P('ch'), may hold values from -3 to 3
- ema_eta: float32 [768, 16], P('ch'), may hold values from -1.5 to 1.5
- ema_omega: float32 [768], P('ch'), may hold values from -2 to 2
- w_mix: bfloat16 [768, 3200], replicated, may hold values from -0.21875 to 0.21875
- b_mix: float32 [3200], replicated, may hold values from -1.5 to 1.5
- w_value: bfloat16 [768, 1536], replicated, may hold values from -0.21875 to 0.21875
- b_value: float32 [1536], replicated, may hold values from -1.5 to 1.5
- w_out: bfloat16 [1536, 768], replicated, may hold values from -0.3125 to 0.3125
- b_out: float32 [768], replicated, may hold values from -1.5 to 1.5
- qk_scale: float32 [2, 128], replicated, may hold values from 0.25 to 1.75
- qk_shift: float32 [2, 128], replicated, may hold values from -1.5 to 1.5
- ln_gain: float32 [768], replicated, may hold values from 0.5 to 1.5
- ln_bias: float32 [768], replicated, may hold values from -1.5 to 1.5
- w_up: bfloat16 [768, 1536], replicated, may hold values from -0.21875 to 0.21875
- b_up: float32 [1536], replicated, may hold values from -1.5 to 1.5
- w_down: bfloat16 [1536, 768], replicated, may hold values from -0.21875 to 0.21875
- b_down: float32 [768], replicated, may hold values from -1.5 to 1.5
Outputs:
- output: bfloat16 [4, 768, 4096], P(None, 'ch', 'tok')
- input_grad: float32 [4, 768, 4096], P(None, 'ch', 'tok')
- grad_ema_alpha: float32 [768, 16], P('ch')
- grad_ema_delta: float32 [768, 16], P('ch')
- grad_ema_beta: float32 [768, 16], P('ch')
- grad_ema_eta: float32 [768, 16], P('ch')
- grad_ema_omega: float32 [768], P('ch')
- grad_w_mix: float32 [768, 3200], P('ch')
- grad_b_mix: float32 [3200], replicated
- grad_w_value: float32 [768, 1536], P('ch')
- grad_b_value: float32 [1536], replicated
- grad_w_out: float32 [1536, 768], P('ch')
- grad_b_out: float32 [768], replicated
- grad_qk_scale: float32 [2, 128], replicated
- grad_qk_shift: float32 [2, 128], replicated
- grad_ln_gain: float32 [768], replicated
- grad_ln_bias: float32 [768], replicated
- grad_w_up: float32 [768, 1536], P('ch')
- grad_b_up: float32 [1536], replicated
- grad_w_down: float32 [1536, 768], P('ch')
- grad_b_down: float32 [768], replicated
Inputs may be any that keep to these rules, and one draw needn't show every extreme that they name: `seq_lengths`: every sequence but one, chosen by the seed, has 4096 live positions; that one has 2560 or more.
All inputs are finite; a program needn't handle non-finite values.
Results may differ from a plain program's by a relative error of at most 0.025.
The roundings to bfloat16 on the way count: a program that leaves them out, or rounds other values in their place, can miss the bound.
Values may be sent and summed in bfloat16 or wider, within the bound.
No kernel may reach another device: no remote copies, remote signals or barrier semaphores. Data moves between devices by JAX's collectives and lax.ppermute only.
A program may use at most 192 MiB of HBM per device.

v0:
```python
import jax
import jax.numpy as jnp
from jax import lax
from jax.sharding import PartitionSpec as P

GROUP = 128
highest = lax.Precision.HIGHEST


def prefix(shard, axis, combine, identity, reverse):
    size, position = (lax.axis_size(axis), lax.axis_index(axis))
    everything = jax.tree.map(lambda part: lax.all_gather(part, axis), shard)
    start = jax.tree.map(
        lambda part, zero: jnp.broadcast_to(jnp.asarray(zero, part.dtype), part.shape),
        shard,
        identity,
    )

    def lap(k, before):
        at = size - 1 - k if reverse else k
        reached = at > position if reverse else at < position
        new = combine(before, jax.tree.map(lambda part: part[at], everything))
        return jax.tree.map(lambda a, b: jnp.where(reached, a, b), new, before)

    return lax.fori_loop(0, size, lap, start)


def silu_slope(preact):
    sigma = jax.nn.sigmoid(preact)
    return sigma * (1.0 + preact * (1.0 - sigma))


def decay_logs(alpha_logit, delta_logit):
    return jnp.log1p(-jax.nn.sigmoid(alpha_logit) * jax.nn.sigmoid(delta_logit))


def ema_core(seq_f, alpha_logit, delta_logit, beta, eta, omega, state_in):
    nseq_count, channels, local_len = seq_f.shape
    blocks_n = local_len // GROUP
    log_decay = decay_logs(alpha_logit, delta_logit)
    scaled = jax.nn.sigmoid(alpha_logit) * beta
    offsets = jnp.arange(GROUP, dtype=jnp.float32)
    powers = jnp.exp(offsets[None, None, :] * log_decay[:, :, None])
    kernel = jnp.einsum("dj,djt->dt", eta * scaled, powers, precision=highest)
    lag = offsets[:, None] - offsets[None, :]
    onehot = (lag[None] == offsets[:, None, None]).astype(jnp.float32)
    toeplitz = jnp.einsum("dm,mts->dts", kernel, onehot, precision=highest)
    blocks = seq_f.reshape(nseq_count, channels, blocks_n, GROUP)
    inner = jnp.einsum("dts,ndbs->ndbt", toeplitz, blocks, precision=highest)
    state_pow = scaled[:, :, None] * jnp.flip(powers, axis=2)
    running = jnp.einsum("djs,ndbs->ndbj", state_pow, blocks, precision=highest)
    span = 1
    while span < blocks_n:
        factor = jnp.exp(span * GROUP * log_decay)
        moved = jnp.pad(running, ((0, 0), (0, 0), (span, 0), (0, 0)))[:, :, :blocks_n]
        running = running + factor[None, :, None, :] * moved
        span = span * 2
    starts = jnp.pad(running, ((0, 0), (0, 0), (1, 0), (0, 0)))[:, :, :blocks_n]
    group_ids = jnp.arange(blocks_n, dtype=jnp.float32)
    entry = jnp.exp(group_ids[None, :, None] * (GROUP * log_decay)[:, None, :])
    starts = starts + entry[None] * state_in[:, :, None, :]
    carry_pow = eta[:, :, None] * powers * jnp.exp(log_decay)[:, :, None]
    smooth = inner + jnp.einsum("djt,ndbj->ndbt", carry_pow, starts, precision=highest)
    smooth = smooth.reshape(nseq_count, channels, local_len)
    return jax.nn.silu(smooth + omega[None, :, None] * seq_f)


def state_advance(seq_f, alpha_logit, delta_logit, beta, state_in):
    local_len = seq_f.shape[2]
    log_decay = decay_logs(alpha_logit, delta_logit)
    scaled = jax.nn.sigmoid(alpha_logit) * beta
    reverse_pos = jnp.arange(local_len - 1, -1, -1, dtype=jnp.float32)
    weights = scaled[:, :, None] * jnp.exp(reverse_pos[None, None, :] * log_decay[:, :, None])
    fresh = jnp.einsum("djs,nds->ndj", weights, seq_f, precision=highest)
    return jnp.exp(local_len * log_decay)[None] * state_in + fresh


def chain_combine(earlier, later):
    return (earlier[0] * later[0], later[0][None] * earlier[1] + later[1])


def to_rows(columns):
    return jnp.swapaxes(columns, 1, 2).reshape(-1, columns.shape[1])


def from_rows(table, nseq_count):
    return jnp.swapaxes(table.reshape(nseq_count, -1, table.shape[1]), 1, 2)


def local(
    inputs,
    out_grad,
    seq_lengths,
    ema_alpha,
    ema_delta,
    ema_beta,
    ema_eta,
    ema_omega,
    w_mix,
    b_mix,
    w_value,
    b_value,
    w_out,
    b_out,
    qk_scale,
    qk_shift,
    ln_gain,
    ln_bias,
    w_up,
    b_up,
    w_down,
    b_down,
):
    nseq_count, channels, local_len = inputs.shape
    width = w_mix.shape[0]
    zwidth = qk_scale.shape[1]
    vwidth = w_value.shape[1]
    scale = zwidth ** (-0.5)
    tok_index = lax.axis_index("tok")
    seq_f = inputs.astype(jnp.float32)
    log_total = local_len * decay_logs(ema_alpha, ema_delta)
    decay_all = jnp.exp(log_total)
    zero_state = jnp.zeros((nseq_count, channels, ema_alpha.shape[1]), jnp.float32)
    state_dev = state_advance(seq_f, ema_alpha, ema_delta, ema_beta, zero_state)
    state_in = prefix(
        (decay_all, state_dev), "tok", chain_combine, (jnp.ones_like(decay_all), zero_state), False
    )[1]
    activ = ema_core(seq_f, ema_alpha, ema_delta, ema_beta, ema_eta, ema_omega, state_in)
    recv_in, recv_mix = (
        lax.all_to_all(inputs, "ch", split_axis=2, concat_axis=1, tiled=True),
        lax.all_to_all(activ.astype(jnp.bfloat16), "ch", split_axis=2, concat_axis=1, tiled=True),
    )
    tok_in = to_rows(recv_in)
    tok_mix = to_rows(recv_mix)
    row_count = tok_in.shape[0]
    blocks_n = row_count // GROUP
    value_pre = jnp.dot(tok_in, w_value, preferred_element_type=jnp.float32) + b_value
    values = jax.nn.silu(value_pre).astype(jnp.bfloat16)
    mix_pre = jnp.dot(tok_mix, w_mix, preferred_element_type=jnp.float32) + b_mix
    gate_pre = mix_pre[:, :width]
    query_pre = mix_pre[:, width : width + zwidth]
    reset_pre = mix_pre[:, width + zwidth : width + zwidth + vwidth]
    hidden_mix = mix_pre[:, width + zwidth + vwidth :]
    update = jax.nn.sigmoid(gate_pre)
    shared = jax.nn.silu(query_pre)
    queries = (shared * qk_scale[0] + qk_shift[0]).astype(jnp.bfloat16)
    keys_all = (shared * qk_scale[1] + qk_shift[1]).astype(jnp.bfloat16)
    reset = jax.nn.silu(reset_pre)
    query_blk = queries.reshape(blocks_n, GROUP, zwidth)
    key_blk = keys_all.reshape(blocks_n, GROUP, zwidth)
    value_blk = values.reshape(blocks_n, GROUP, vwidth)
    position = jnp.arange(GROUP)
    causal = position[:, None] >= position[None, :]

    def block_scores():
        raw = (
            jnp.einsum("cqz,ckz->cqk", query_blk, key_blk, preferred_element_type=jnp.float32)
            * scale
        )
        return jnp.where(causal[None], raw, -1e30)

    scores = block_scores()
    top_score = jnp.max(scores, axis=-1, keepdims=True)
    log_norm = top_score + jnp.log(jnp.sum(jnp.exp(scores - top_score), axis=-1, keepdims=True))
    probs_bf = jnp.exp(scores - log_norm).astype(jnp.bfloat16)
    attended = jnp.einsum(
        "cqk,ckv->cqv", probs_bf, value_blk, preferred_element_type=jnp.float32
    ).reshape(row_count, vwidth)
    gated = (reset * attended).astype(jnp.bfloat16)
    hidden_pre = hidden_mix + jnp.dot(gated, w_out, preferred_element_type=jnp.float32) + b_out
    hidden = jax.nn.silu(hidden_pre)
    resid = tok_in.astype(jnp.float32)
    blend = update * hidden + (1.0 - update) * resid
    centered = blend - jnp.mean(blend, axis=-1, keepdims=True)
    rstd = lax.rsqrt(jnp.mean(centered * centered, axis=-1, keepdims=True) + 1e-05)
    unit = centered * rstd
    normed = unit * ln_gain + ln_bias
    normed_bf = normed.astype(jnp.bfloat16)
    ffn_pre = jnp.dot(normed_bf, w_up, preferred_element_type=jnp.float32) + b_up
    ffn_hidden = jax.nn.silu(ffn_pre).astype(jnp.bfloat16)
    result = normed + jnp.dot(ffn_hidden, w_down, preferred_element_type=jnp.float32) + b_down
    out_local = lax.all_to_all(
        from_rows(result.astype(jnp.bfloat16), nseq_count),
        "ch",
        split_axis=1,
        concat_axis=2,
        tiled=True,
    )
    seq_pos = tok_index * local_len + jnp.arange(local_len, dtype=jnp.int32)
    live = (seq_pos[None, :] < seq_lengths[:, None])[:, None, :]
    output = jnp.where(live, out_local, jnp.zeros_like(out_local))
    grad_masked = jnp.where(live, out_grad, jnp.zeros_like(out_grad))
    grad_rows = to_rows(lax.all_to_all(grad_masked, "ch", split_axis=2, concat_axis=1, tiled=True))
    grad_f = grad_rows.astype(jnp.float32)
    g_down = jnp.dot(ffn_hidden.T, grad_rows, preferred_element_type=jnp.float32)
    g_bdown = jnp.sum(grad_f, axis=0)
    d_ffn = (
        jnp.dot(grad_rows, w_down.T, preferred_element_type=jnp.float32) * silu_slope(ffn_pre)
    ).astype(jnp.bfloat16)
    g_up = jnp.dot(normed_bf.T, d_ffn, preferred_element_type=jnp.float32)
    g_bup = jnp.sum(d_ffn.astype(jnp.float32), axis=0)
    d_normed = grad_f + jnp.dot(d_ffn, w_up.T, preferred_element_type=jnp.float32)
    g_gain = jnp.sum(d_normed * unit, axis=0)
    g_lnbias = jnp.sum(d_normed, axis=0)
    d_unit = d_normed * ln_gain
    d_blend = rstd * (
        d_unit
        - jnp.mean(d_unit, axis=-1, keepdims=True)
        - unit * jnp.mean(d_unit * unit, axis=-1, keepdims=True)
    )
    d_hidden_pre = (d_blend * update * silu_slope(hidden_pre)).astype(jnp.bfloat16)
    d_update_pre = d_blend * (hidden - resid) * update * (1.0 - update)
    d_direct = d_blend * (1.0 - update)
    g_out = jnp.dot(gated.T, d_hidden_pre, preferred_element_type=jnp.float32)
    g_bout = jnp.sum(d_hidden_pre.astype(jnp.float32), axis=0)
    d_gated = jnp.dot(d_hidden_pre, w_out.T, preferred_element_type=jnp.float32)
    d_reset_pre = d_gated * attended * silu_slope(reset_pre)
    d_attended = (d_gated * reset).astype(jnp.bfloat16).reshape(blocks_n, GROUP, vwidth)
    scores = block_scores()
    probs = jnp.exp(scores - log_norm)
    probs_bf = probs.astype(jnp.bfloat16)
    d_probs = jnp.einsum("cqv,ckv->cqk", d_attended, value_blk, preferred_element_type=jnp.float32)
    d_values = jnp.einsum(
        "cqk,cqv->ckv", probs_bf, d_attended, preferred_element_type=jnp.float32
    ).reshape(row_count, vwidth)
    d_scores = (probs * (d_probs - jnp.sum(d_probs * probs, axis=-1, keepdims=True))).astype(
        jnp.bfloat16
    )
    d_query = (
        jnp.einsum("cqk,ckz->cqz", d_scores, key_blk, preferred_element_type=jnp.float32).reshape(
            row_count, zwidth
        )
        * scale
    )
    d_key = (
        jnp.einsum("cqk,cqz->ckz", d_scores, query_blk, preferred_element_type=jnp.float32).reshape(
            row_count, zwidth
        )
        * scale
    )
    d_value_pre = (d_values * silu_slope(value_pre)).astype(jnp.bfloat16)
    g_value = jnp.dot(tok_in.T, d_value_pre, preferred_element_type=jnp.float32)
    g_bvalue = jnp.sum(d_value_pre.astype(jnp.float32), axis=0)
    d_resid = d_direct + jnp.dot(d_value_pre, w_value.T, preferred_element_type=jnp.float32)
    g_qscale = jnp.stack([jnp.sum(d_query * shared, axis=0), jnp.sum(d_key * shared, axis=0)])
    g_qshift = jnp.stack([jnp.sum(d_query, axis=0), jnp.sum(d_key, axis=0)])
    d_query_pre = (d_query * qk_scale[0] + d_key * qk_scale[1]) * silu_slope(query_pre)
    d_mix_pre = jnp.concatenate(
        [d_update_pre, d_query_pre, d_reset_pre, d_hidden_pre.astype(jnp.float32)], axis=1
    ).astype(jnp.bfloat16)
    g_mix = jnp.dot(tok_mix.T, d_mix_pre, preferred_element_type=jnp.float32)
    g_bmix = jnp.sum(d_mix_pre.astype(jnp.float32), axis=0)
    d_mix_in = jnp.dot(d_mix_pre, w_mix.T, preferred_element_type=jnp.float32)
    back_resid, back_mix = (
        lax.all_to_all(
            from_rows(d_resid.astype(jnp.bfloat16), nseq_count),
            "ch",
            split_axis=1,
            concat_axis=2,
            tiled=True,
        ),
        lax.all_to_all(
            from_rows(d_mix_in.astype(jnp.bfloat16), nseq_count),
            "ch",
            split_axis=1,
            concat_axis=2,
            tiled=True,
        ),
    )
    _, ema_pull = jax.vjp(
        ema_core, seq_f, ema_alpha, ema_delta, ema_beta, ema_eta, ema_omega, state_in
    )
    dx_ema, ga_first, gd_first, gb_first, g_eta, g_omega, state_grad = ema_pull(
        back_mix.astype(jnp.float32)
    )
    later_grad = prefix(
        (decay_all, state_grad), "tok", chain_combine, (jnp.ones_like(decay_all), zero_state), True
    )[1]
    _, state_pull = jax.vjp(state_advance, seq_f, ema_alpha, ema_delta, ema_beta, state_in)
    dx_state, ga_second, gd_second, gb_second, unused_grad = state_pull(later_grad)
    input_grad = back_resid.astype(jnp.float32) + dx_ema + dx_state
    g_mix_s, g_value_s, g_out_s, g_up_s, g_down_s = (
        lax.psum_scatter(g_mix, "ch", scatter_dimension=0, tiled=True),
        lax.psum_scatter(g_value, "ch", scatter_dimension=0, tiled=True),
        lax.psum_scatter(g_out, "ch", scatter_dimension=0, tiled=True),
        lax.psum_scatter(g_up, "ch", scatter_dimension=0, tiled=True),
        lax.psum_scatter(g_down, "ch", scatter_dimension=0, tiled=True),
    )
    summed = lax.psum(
        (
            g_mix_s,
            g_value_s,
            g_out_s,
            g_up_s,
            g_down_s,
            ga_first + ga_second,
            gd_first + gd_second,
            gb_first + gb_second,
            g_eta,
            g_omega,
        ),
        "tok",
    )
    smalls = lax.psum(
        (g_bmix, g_bvalue, g_bout, g_qscale, g_qshift, g_gain, g_lnbias, g_bup, g_bdown),
        ("ch", "tok"),
    )
    return (
        output,
        input_grad,
        summed[5],
        summed[6],
        summed[7],
        summed[8],
        summed[9],
        summed[0],
        smalls[0],
        summed[1],
        smalls[1],
        summed[2],
        smalls[2],
        smalls[3],
        smalls[4],
        smalls[5],
        smalls[6],
        summed[3],
        smalls[7],
        summed[4],
        smalls[8],
    )


def solution(mesh):
    placed = (
        P(None, "ch", "tok"),
        P(None, "ch", "tok"),
        P(),
        P("ch", None),
        P("ch", None),
        P("ch", None),
        P("ch", None),
        P("ch"),
        P(),
        P(),
        P(),
        P(),
        P(),
        P(),
        P(),
        P(),
        P(),
        P(),
        P(),
        P(),
        P(),
        P(),
    )
    return jax.shard_map(
        local,
        mesh=mesh,
        in_specs=placed,
        out_specs=(
            P(None, "ch", "tok"),
            P(None, "ch", "tok"),
            P("ch", None),
            P("ch", None),
            P("ch", None),
            P("ch", None),
            P("ch"),
            P("ch", None),
            P(),
            P("ch", None),
            P(),
            P("ch", None),
            P(),
            P(),
            P(),
            P(),
            P(),
            P("ch", None),
            P(),
            P("ch", None),
            P(),
        ),
        check_vma=False,
    )
```

profile of v0, /device:TPU:0, one launch (start us, length us, event | category | flops | bytes accessed | tf_op | source)
XLA Modules:
  0.0 922.5 jit_solution(10097495097072046068)
XLA Ops:
  9.8 7.3 all-to-all-start.1
  21.9 5.6 all-gather.3
  30.5 5.1 fusion.73
  35.7 5.9 all-gather.1
  41.6 7.6 while.30
  59.5 5.2 fusion.28
  68.4 3.5 fusion.77
  71.9 10.1 %bitcast_add_fusion.3 = f32[4,96,8,128]{3,2,0,1:T(8,128)} fusion(f32[96,4,8,128]{3,2,1,0:T(8,128)S(1)} %fusion.77, f32[96,128,128,1]{2,0,1,3:T(8,128)} %fusion.28, bf16[4,96,8,128]{3,2,1,0:T(8,128)(2,1)S(1)} %bitcast.299), kind=kOutput, calls=%fused_computation.96 | convolution fusion | flops 604372992 | bytes 10223616 | tf_op jit(solution)/shard_map/dts,ndbs->ndbt/dot_general | solution.py:49
  84.7 3.5 multiply_convert_fusion.4
  88.3 3.5 copy.343
  91.7 6.2 all-to-all-start
  103.3 21.0 %all-to-all-done = bf16[4,96,1024]{1,0,2:T(4,128)(2,1)} async-done(((bf16[4,96,1024]{1,0,2:T(4,128)(2,1)}), bf16[4,96,1024]{1,0,2:T(4,128)(2,1)}, u32[]{:S(2)}, u32[]{:S(2)}) %all-to-all-start) | async-done | bytes 786464 | tf_op jit(solution)/shard_map/all_to_all | solution.py:131
  129.0 5.6 convolution_add_fusion
  135.5 3.3 multiply_convert_fusion.2
  152.7 4.2 all-to-all-start.2
  158.5 18.4 %all-to-all-done.2 = bf16[4,768,128]{2,0,1:T(4,128)(2,1)} async-done(((bf16[4,768,128]{2,0,1:T(4,128)(2,1)}), bf16[4,768,128]{2,0,1:T(4,128)(2,1)}, u32[]{:S(2)}, u32[]{:S(2)}) %all-to-all-start.2) | async-done | bytes 786464 | tf_op jit(solution)/shard_map/all_to_all | solution.py:182
  181.8 29.6 %all_to_all.90 = bf16[4,96,1024]{1,0,2:T(4,128)(2,1)} all-to-all(bf16[4,96,1024]{1,0,2:T(4,128)(2,1)} %copy.355), channel_id=1, replica_groups=mesh['ch'=8,'tok'=4] {'ch'}, dimensions={2} | all-to-all | bytes 1572864 | tf_op jit(solution)/shard_map/all_to_all | solution.py:193
  216.1 5.6 convert_reduce_fusion.1
  224.1 4.8 convert_reduce_fusion.4
  228.9 5.6 fusion.19
  238.8 3.6 convolution_bitcast_fusion
  242.4 6.0 copy.413
  249.6 5.6 fusion.145
  255.9 5.6 fusion.142
  262.6 4.9 fusion.159
  273.9 6.5 fusion.146
  280.5 6.9 convolution_convert_fusion
  289.6 4.2 all-to-all-start.5
  293.8 5.8 add_convert_fusion
  301.8 11.5 %all-to-all-done.5 = bf16[4,768,128]{2,0,1:T(4,128)(2,1)} async-done(((bf16[4,768,128]{2,0,1:T(4,128)(2,1)}), bf16[4,768,128]{2,0,1:T(4,128)(2,1)}, u32[]{:S(2)}, u32[]{:S(2)}) %all-to-all-start.5) | async-done | bytes 786464 | tf_op jit(solution)/shard_map/all_to_all | solution.py:262
  313.3 4.4 all-to-all-start.4
  323.8 46.7 %all-reduce.8 = (f32[3200]{0:T(1024)}, f32[1536]{0:T(1024)}, f32[768]{0:T(1024)}, f32[2,128]{1,0:T(2,128)}, f32[2,128]{1,0:T(2,128)}, /*index=5*/f32[768]{0:T(10...) all-reduce(f32[3200]{0:T(1024)S(1)} %convert_reduce_fusion, ...), channel_id=1, replica_groups=mesh['ch'=8,'tok'=4] {'ch','tok'}, use_global_device_ids=true, to_apply=%region_33.34 | all-reduce | flops 9856 | bytes 78848 | tf_op jit(solution)/shard_map/psum | solution.py:304
  383.1 5.1 fusion.30
  395.3 3.7 multiply_reduce_fusion.6
  399.0 6.0 all-gather.2
  412.9 11.1 %add_bitcast_fusion = f32[4,96,8,128]{3,2,0,1:T(8,128)} fusion(f32[96,4,8,128]{3,2,1,0:T(8,128)S(1)} %fusion.80, f32[96,128,128,1]{2,0,1,3:T(8,128)} %fusion.28, f32[4,96,8,128]{3,2,0,1:T(8,128)S(1)} %copy-done.11), kind=kOutput, calls=%fused_computation.105 | convolution fusion | flops 604372992 | bytes 11010048 | tf_op jit(solution)/shard_map/transpose(jvp(dts,ndbs->ndbt))/dot_general | solution.py:49
  427.3 4.8 multiply_reduce_fusion.14
  432.2 5.1 bitcast_add_fusion.2
  437.2 6.2 multiply_reduce_fusion
  445.7 10.9 %reduce-scatter.14.cloned.1.call-done = f32[192,768]{1,0:T(8,128)} async-done(((f32[1536,768]{1,0:T(8,128)}), f32[192,768]{1,0:T(8,128)}) %reduce-scatter.14.cloned.1.call-update) | async-done | bytes 589840 | tf_op jit(solution)/shard_map/reduce_scatter | solution.py:287
  456.5 98.7 %reduce-scatter.12.cloned.1.call-done = f32[96,1536]{1,0:T(8,128)} async-done(((f32[768,1536]{1,0:T(8,128)}), f32[96,1536]{1,0:T(8,128)}) %reduce-scatter.12.cloned.1.call-update) | async-done | bytes 589840 | tf_op jit(solution)/shard_map/reduce_scatter | solution.py:286
  555.2 98.5 %reduce-scatter.10.cloned.1.call-done = f32[192,768]{1,0:T(8,128)} async-done(((f32[1536,768]{1,0:T(8,128)}), f32[192,768]{1,0:T(8,128)}) %reduce-scatter.10.cloned.1.call-update) | async-done | bytes 589840 | tf_op jit(solution)/shard_map/reduce_scatter | solution.py:285
  653.8 172.3 %reduce-scatter.8.cloned.1.call-done = f32[96,3200]{1,0:T(8,128)} async-done(((f32[768,3200]{1,0:T(8,128)}), f32[96,3200]{1,0:T(8,128)}) %reduce-scatter.8.cloned.1.call-update) | async-done | bytes 1228816 | tf_op jit(solution)/shard_map/reduce_scatter | solution.py:283
  835.1 5.1 convolution_bitcast_fusion.1
  840.3 7.9 fusion.2
  849.9 5.5 multiply_reduce_fusion.11
  856.6 13.3 %all-reduce.9 = (f32[96,16]{0,1:T(8,128)}, f32[96,16]{0,1:T(8,128)}, f32[96,16]{0,1:T(8,128)}, f32[96,16]{0,1:T(8,128)}, f32[96]{0:T(128)}) all-reduce(f32[96,16]{0,1:T(8,128)S(1)} %get-tuple-element.526, f32[96,16]{0,1:T(8,128)S(1)} %get-tuple-element.525, ...), channel_id=1, replica_groups=mesh['ch'=8,'tok'=4] {'tok'}, use_global_device_ids=true, to_apply=%region_23.24 | all-reduce | flops 6240 | bytes 49920 | tf_op jit(solution)/shard_map/psum | solution.py:289
  869.8 38.4 %all-reduce.13.cloned.1.call-done = (f32[96,3200]{1,0:T(8,128)}, f32[96,1536]{0,1:T(8,128)}, f32[192,768]{1,0:T(8,128)}, f32[96,1536]{1,0:T(8,128)}, f32[192,768]{1,0:T(8,128)}) async-done(((f32[96,3200]{1,0:T(8,128)}, f32[96,1536]{0,1:T(8,128)}, f32[192,768]{1,0:T(8,128)}, f32[96,1536]{1,0:T(8,128)}, f32[192,768]{1,0:T(8,128)}), (f32[96,3200]{1,0:T(8,128)}, f32[96,1536]{0,1:T(8,128)}, ...) | async-done | bytes 3588112 | tf_op jit(solution)/shard_map/psum | solution.py:289
  (429 shorter events, 151.2 us)
Async XLA Ops:
  7.2 135.0 %copy-start = (bf16[1536,768]{1,0:T(8,128)(2,1)S(1)}, bf16[1536,768]{1,0:T(8,128)(2,1)}, u32[]{:S(2)}) copy-start(bf16[1536,768]{1,0:T(8,128)(2,1)} %param.38) | copy-start | bytes 7077892
  7.2 10.4 %copy-start.84 = (f32[96,16]{0,1:T(8,128)S(1)}, f32[96,16]{0,1:T(8,128)}, u32[]{:S(2)}) copy-start(f32[96,16]{0,1:T(8,128)} %param.32) | copy-start | bytes 18436
  7.2 10.4 %copy-start.99 = (f32[96,16]{0,1:T(8,128)S(1)}, f32[96,16]{0,1:T(8,128)}, u32[]{:S(2)}) copy-start(f32[96,16]{0,1:T(8,128)} %param.31) | copy-start | bytes 18436
  7.2 10.4 %copy-start.103 = (f32[96,16]{0,1:T(8,128)S(1)}, f32[96,16]{0,1:T(8,128)}, u32[]{:S(2)}) copy-start(f32[96,16]{0,1:T(8,128)} %param.30) | copy-start | bytes 18436
  7.2 10.4 %copy-start.101 = (f32[96,16]{0,1:T(8,128)S(1)}, f32[96,16]{0,1:T(8,128)}, u32[]{:S(2)}) copy-start(f32[96,16]{0,1:T(8,128)} %param.29) | copy-start | bytes 18436
  9.8 82.0 %all-to-all-start.1 = ((bf16[4,96,1024]{1,0,2:T(4,128)(2,1)}), bf16[4,96,1024]{1,0,2:T(4,128)(2,1)}, u32[]{:S(2)}, u32[]{:S(2)}) async-start(bf16[4,96,1024]{1,0,2:T(4,128)(2,1)} %copy.347), calls=%async_computation.1 | async-start | bytes 2097152 | tf_op jit(solution)/shard_map/all_to_all | solution.py:130
  17.0 13.5 %copy-start.15 = (bf16[4,96,1024]{2,1,0:T(8,128)(2,1)S(1)}, bf16[4,96,1024]{2,1,0:T(8,128)(2,1)}, u32[]{:S(2)}) copy-start(bf16[4,96,1024]{2,1,0:T(8,128)(2,1)} %param.26) | copy-start | bytes 2359300
  18.3 12.1 %copy-start.86 = (f32[96,16]{0,1:T(8,128)}, f32[96,16]{0,1:T(8,128)S(1)}, u32[]{:S(2)}) copy-start(f32[96,16]{0,1:T(8,128)S(1)} %get-tuple-element.512) | copy-start | bytes 18436
  18.4 17.2 %copy-start.54 = (f32[96,16]{1,0:T(8,128)}, f32[96,16]{1,0:T(8,128)S(1)}, u32[]{:S(2)}) copy-start(f32[96,16]{1,0:T(8,128)S(1)} %copy.325) | copy-start | bytes 18436
  19.2 16.4 %copy-start.51 = (f32[96,16]{1,0:T(8,128)}, f32[96,16]{1,0:T(8,128)S(1)}, u32[]{:S(2)}) copy-start(f32[96,16]{1,0:T(8,128)S(1)} %copy.328) | copy-start | bytes 18436
  50.0 18.4 %copy-start.31 = (f32[96,8,16]{2,1,0:T(8,128)}, f32[96,8,16]{2,1,0:T(8,128)S(1)}, u32[]{:S(2)}) copy-start(f32[96,8,16]{2,1,0:T(8,128)S(1)} %multiply_exponential_fusion.4) | copy-start | bytes 147460
  88.3 10.3 %copy-start.120 = (f32[2,128]{1,0:T(2,128)S(1)}, f32[2,128]{1,0:T(2,128)}, u32[]{:S(2)}) copy-start(f32[2,128]{1,0:T(2,128)} %param.40) | copy-start | bytes 3076
  88.3 10.3 %copy-start.126 = (f32[2,128]{1,0:T(2,128)S(1)}, f32[2,128]{1,0:T(2,128)}, u32[]{:S(2)}) copy-start(f32[2,128]{1,0:T(2,128)} %param.41) | copy-start | bytes 3076
  91.7 32.5 %all-to-all-start = ((bf16[4,96,1024]{1,0,2:T(4,128)(2,1)}), bf16[4,96,1024]{1,0,2:T(4,128)(2,1)}, u32[]{:S(2)}, u32[]{:S(2)}) async-start(bf16[4,96,1024]{1,0,2:T(4,128)(2,1)} %copy.343), calls=%async_computation | async-start | bytes 2097152 | tf_op jit(solution)/shard_map/all_to_all | solution.py:131
  128.9 6.6 copy-start.23
  128.9 6.6 copy-start.130
  134.6 6.9 copy-start.30
  152.7 24.2 %all-to-all-start.2 = ((bf16[4,768,128]{2,0,1:T(4,128)(2,1)}), bf16[4,768,128]{2,0,1:T(4,128)(2,1)}, u32[]{:S(2)}, u32[]{:S(2)}) async-start(bf16[4,768,128]{2,0,1:T(4,128)(2,1)} %bitcast.313), calls=%async_computation.2 | async-start | bytes 1572864 | tf_op jit(solution)/shard_map/all_to_all | solution.py:182
  156.9 286.6 %reduce-scatter.16.cloned.1.call-start = ((), (), s32[]{:S(2)}) async-start(), calls=%async_computation.15 | async-start | bytes 5308416
  248.4 208.1 %reduce-scatter.14.cloned.1.call-start = ((), (), s32[]{:S(2)}) async-start(), calls=%async_computation.14 | async-start | bytes 5308416 | tf_op jit(solution)/shard_map/reduce_scatter | solution.py:287
  255.2 300.0 %reduce-scatter.12.cloned.1.call-start = ((), (), s32[]{:S(2)}) async-start(), calls=%async_computation.13 | async-start | bytes 5308416 | tf_op jit(solution)/shard_map/reduce_scatter | solution.py:286
  261.5 392.2 %reduce-scatter.10.cloned.1.call-start = ((), (), s32[]{:S(2)}) async-start(), calls=%async_computation.12 | async-start | bytes 5308416 | tf_op jit(solution)/shard_map/reduce_scatter | solution.py:285
  267.6 558.4 %reduce-scatter.8.cloned.1.call-start = ((), (), s32[]{:S(2)}) async-start(), calls=%async_computation.11 | async-start | bytes 11059200 | tf_op jit(solution)/shard_map/reduce_scatter | solution.py:283
  289.6 23.7 %all-to-all-start.5 = ((bf16[4,768,128]{2,0,1:T(4,128)(2,1)}), bf16[4,768,128]{2,0,1:T(4,128)(2,1)}, u32[]{:S(2)}, u32[]{:S(2)}) async-start(bf16[4,768,128]{2,0,1:T(4,128)(2,1)} %bitcast.312), calls=%async_computation.5 | async-start | bytes 1572864 | tf_op jit(solution)/shard_map/all_to_all | solution.py:262
  313.3 8.4 copy-start.121
  313.3 8.5 copy-start.122
  313.3 8.5 copy-start.20
  313.3 63.4 %all-to-all-start.4 = ((bf16[4,768,128]{2,0,1:T(4,128)(2,1)}), bf16[4,768,128]{2,0,1:T(4,128)(2,1)}, u32[]{:S(2)}, u32[]{:S(2)}) async-start(bf16[4,768,128]{2,0,1:T(4,128)(2,1)} %bitcast.48), calls=%async_computation.4 | async-start | bytes 1572864 | tf_op jit(solution)/shard_map/all_to_all | solution.py:255
  317.7 590.5 %all-reduce.13.cloned.1.call-start = ((), (), s32[]{:S(2)}) async-start(), calls=%async_computation.16 | async-start | bytes 7569408 | tf_op jit(solution)/shard_map/psum | solution.py:289
  395.3 9.8 %copy-start.40 = (f32[4,96,16]{1,2,0:T(8,128)S(1)}, f32[4,96,16]{1,2,0:T(8,128)}, u32[]{:S(2)}) copy-start(f32[4,96,16]{1,2,0:T(8,128)} %custom-call.1) | copy-start | bytes 73732
  840.2 8.0 copy-start.57
  840.2 9.5 %copy-start.39 = (f32[4,96,16]{2,0,1:T(4,128)S(1)}, f32[4,96,16]{2,0,1:T(4,128)}, u32[]{:S(2)}) copy-start(f32[4,96,16]{2,0,1:T(4,128)} %copy.339) | copy-start | bytes 73732
  840.2 9.5 %copy-start.61 = (f32[96,16,128]{2,1,0:T(8,128)S(1)}, f32[96,16,128]{2,1,0:T(8,128)}, u32[]{:S(2)}) copy-start(f32[96,16,128]{2,1,0:T(8,128)} %rev.11) | copy-start | bytes 2359300
  840.2 9.5 %copy-start.69 = (f32[96,16]{1,0:T(8,128)S(1)}, f32[96,16]{1,0:T(8,128)}, u32[]{:S(2)}) copy-start(f32[96,16]{1,0:T(8,128)} %copy.340) | copy-start | bytes 18436
  840.3 9.5 %copy-start.71 = (f32[96,16]{1,0:T(8,128)S(1)}, f32[96,16]{1,0:T(8,128)}, u32[]{:S(2)}) copy-start(f32[96,16]{1,0:T(8,128)} %copy.341) | copy-start | bytes 18436
  840.3 9.5 %copy-start.90 = (f32[96,16]{1,0:T(8,128)S(1)}, f32[96,16]{1,0:T(8,128)}, u32[]{:S(2)}) copy-start(f32[96,16]{1,0:T(8,128)} %copy.378) | copy-start | bytes 18436
  849.8 6.6 copy-start.83
  849.8 6.6 copy-start.85
  849.8 6.6 copy-start.87
  849.8 6.6 copy-start.94
  849.8 6.6 copy-start.95
  849.8 6.6 copy-start.96
  849.8 6.6 copy-start.97
  849.8 6.6 copy-start.98
  849.9 6.6 copy-start.100
  849.9 6.6 copy-start.102
  849.9 6.6 copy-start.104
  849.9 6.7 copy-start.123
  (103 other events, 278.0 us)
Sparse Core Ops, SparseCore 0:
  248.6 109.6 reduce-scatter.15
  362.0 94.5 reduce-scatter.13
  460.2 94.9 reduce-scatter.11
  558.7 94.9 reduce-scatter.9
  657.3 168.7 reduce-scatter.7
  828.6 79.5 all-reduce.12
where the time goes:
time: 930 us; the launch traced here: 922 us
  waiting for transfers between devices  470 us (51%)
  matrix products  152 us (16%)
  local copies, waits for them, and re-layouts  108 us (12%)
  blocking collectives  107 us (12%)
  other arithmetic  43.4 us (5%)
  starting transfers between devices  27.3 us (3%)
  between operations  15.8 us (2%)
    reduce_scatter x1, waiting for transfers between devices, local(): lax.psum_scatter(g_mix, 'ch', scatter_dimension=0, tiled=True)  172 us
    reduce_scatter x1, waiting for transfers between devices, local(): lax.psum_scatter(g_up, 'ch', scatter_dimension=0, tiled=True)  98.7 us
    reduce_scatter x1, waiting for transfers between devices, local(): lax.psum_scatter(g_out, 'ch', scatter_dimension=0, tiled=True)  98.5 us
    psum x1, blocking collectives, local(): lax.psum((g_bmix, g_bvalue, g_bout, g_qscale, g_qshift, g_gain, g_lnbias,...  46.7 us
    psum x1, waiting for transfers between devices, local(): lax.psum((g_mix_s, g_value_s, g_out_s, g_up_s, g_down_s, ga_first + ga_se...  38.4 us
    unnamed x291, local copies, waits for them, and re-layouts  36.5 us
    all_to_all x1, blocking collectives, local(): lax.all_to_all(grad_masked, 'ch', split_axis=2, concat_axis=1, tiled=True)  29.6 us
    dot_general x3, matrix products, ema_core(): inner = jnp.einsum('dts,ndbs->ndbt', toeplitz, blocks, precision=highest)  26.3 us
  transfers between devices with their start and end apart: 11, of which 8 were waited for; matrix products, arithmetic and copies ran while one was open for 23% of the time, Pallas kernels for 0%

commit v1 on v0

--- a/solution.py
+++ b/solution.py
@@ -179,13 +179,20 @@
     ffn_pre = jnp.dot(normed_bf, w_up, preferred_element_type=jnp.float32) + b_up
     ffn_hidden = jax.nn.silu(ffn_pre).astype(jnp.bfloat16)
     result = normed + jnp.dot(ffn_hidden, w_down, preferred_element_type=jnp.float32) + b_down
-    out_local = lax.all_to_all(
-        from_rows(result.astype(jnp.bfloat16), nseq_count),
-        "ch",
-        split_axis=1,
-        concat_axis=2,
-        tiled=True,
-    )
+    x = from_rows(result.astype(jnp.bfloat16), nseq_count)
+    ways, here = (lax.axis_size("ch"), lax.axis_index("ch"))
+    width_2 = x.shape[1] // ways
+    shape = list(x.shape)
+    shape[1] = width_2
+    height = shape[2]
+    shape[2] = height * ways
+    full = jnp.zeros(shape, x.dtype)
+    for mask in range(ways):
+        part_2 = lax.dynamic_slice_in_dim(x, (here ^ mask) * width_2, width_2, axis=1)
+        if mask:
+            part_2 = lax.ppermute(part_2, "ch", [(d, d ^ mask) for d in range(ways)])
+        full = lax.dynamic_update_slice_in_dim(full, part_2, (here ^ mask) * height, axis=2)
+    out_local = full
     seq_pos = tok_index * local_len + jnp.arange(local_len, dtype=jnp.int32)
     live = (seq_pos[None, :] < seq_lengths[:, None])[:, None, :]
     output = jnp.where(live, out_local, jnp.zeros_like(out_local))

time: 930 us -> 930 us (level)
    all_to_all x1 -> x0, waiting for transfers between devices: 18.4 us -> none  [local(): lax.all_to_all(from_rows(result.astype(jnp.bfloat16), nseq_count), 'ch',...]
    ppermute x0 -> x7, waiting for transfers between devices: none -> 14.6 us  [local(): part_2 = lax.ppermute(part_2, 'ch', [(d, d ^ mask) for d in range(ways)])]
    ppermute x0 -> x7, starting transfers between devices: none -> 10.2 us  [local(): part_2 = lax.ppermute(part_2, 'ch', [(d, d ^ mask) for d in range(ways)])]
    unnamed x291 -> x302, local copies, waits for them, and re-layouts: 36.5 us -> 42 us
  transfers between devices with their start and end apart: 11 -> 17, of which waited for: 8 -> 10; matrix products, arithmetic and copies ran while one was open for 23% -> 24% of each run, Pallas kernels for 0% -> 0%
where the time goes in v1:
time: 930 us; the launch traced here: 922 us
  waiting for transfers between devices  462 us (50%)
  matrix products  151 us (16%)
  local copies, waits for them, and re-layouts  109 us (12%)
  blocking collectives  106 us (11%)
  other arithmetic  45.8 us (5%)
  starting transfers between devices  32.9 us (4%)
  between operations  16 us (2%)
    reduce_scatter x1, waiting for transfers between devices, local(): lax.psum_scatter(g_mix, 'ch', scatter_dimension=0, tiled=True)  172 us
    reduce_scatter x1, waiting for transfers between devices, local(): lax.psum_scatter(g_up, 'ch', scatter_dimension=0, tiled=True)  98.7 us
    reduce_scatter x1, waiting for transfers between devices, local(): lax.psum_scatter(g_out, 'ch', scatter_dimension=0, tiled=True)  98.7 us
    psum x1, blocking collectives, local(): lax.psum((g_bmix, g_bvalue, g_bout, g_qscale, g_qshift, g_gain, g_lnbias,...  44.4 us
    unnamed x302, local copies, waits for them, and re-layouts  42 us
    psum x1, waiting for transfers between devices, local(): lax.psum((g_mix_s, g_value_s, g_out_s, g_up_s, g_down_s, ga_first + ga_se...  38.3 us
    all_to_all x1, blocking collectives, local(): lax.all_to_all(grad_masked, 'ch', split_axis=2, concat_axis=1, tiled=True)  30.3 us
    dot_general x3, matrix products, ema_core(): inner = jnp.einsum('dts,ndbs->ndbt', toeplitz, blocks, precision=highest)  26.3 us
  transfers between devices with their start and end apart: 17, of which 10 were waited for; matrix products, arithmetic and copies ran while one was open for 24% of the time, Pallas kernels for 0%

profile of v1, /device:TPU:0, one launch (start us, length us, event | category | flops | bytes accessed | tf_op | source)
XLA Modules:
  0.0 922.2 jit_solution(14887608952919083874)
XLA Ops:
  9.8 7.3 all-to-all-start.1
  21.9 5.6 all-gather.3
  30.5 5.1 fusion.73
  35.7 5.9 all-gather.1
  41.6 7.5 while.30
  59.5 5.1 fusion.28
  68.2 3.5 fusion.77
  71.7 10.1 %bitcast_add_fusion.3 = f32[4,96,8,128]{3,2,0,1:T(8,128)} fusion(f32[96,4,8,128]{3,2,1,0:T(8,128)S(1)} %fusion.77, f32[96,128,128,1]{2,0,1,3:T(8,128)} %fusion.28, bf16[4,96,8,128]{3,2,1,0:T(8,128)(2,1)S(1)} %bitcast.317), kind=kOutput, calls=%fused_computation.96 | convolution fusion | flops 604372992 | bytes 10223616 | tf_op jit(solution)/shard_map/dts,ndbs->ndbt/dot_general | solution.py:49
  84.6 3.5 multiply_convert_fusion.4
  88.1 3.4 copy.381
  91.6 6.1 all-to-all-start
  106.3 17.8 %all-to-all-done = bf16[4,96,1024]{1,0,2:T(4,128)(2,1)} async-done(((bf16[4,96,1024]{1,0,2:T(4,128)(2,1)}), bf16[4,96,1024]{1,0,2:T(4,128)(2,1)}, u32[]{:S(2)}, u32[]{:S(2)}) %all-to-all-start) | async-done | bytes 786464 | tf_op jit(solution)/shard_map/all_to_all | solution.py:131
  128.9 5.6 convolution_add_fusion
  163.2 9.9 %collective-permute-done.3 = bf16[4,96,128]{1,0,2:T(4,128)(2,1)S(1)} collective-permute-done((bf16[4,96,128]{1,0,2:T(4,128)(2,1)S(1)}, bf16[4,96,128]{1,0,2:T(4,128)(2,1)S(1)}, u32[]{:S(2)}, u32[]{:S(2)}) %collective-permute-start.3) | collective-permute-done | bytes 98336 | tf_op jit(solution)/shard_map/ppermute | solution.py:193
  173.1 3.6 collective-permute-done.4
  177.0 4.2 broadcast_select_fusion
  181.2 30.3 %all_to_all.72 = bf16[4,96,1024]{1,0,2:T(4,128)(2,1)} all-to-all(bf16[4,96,1024]{1,0,2:T(4,128)(2,1)S(1)} %get-tuple-element.533), channel_id=1, replica_groups=mesh['ch'=8,'tok'=4] {'ch'}, dimensions={2} | all-to-all | bytes 1572864 | tf_op jit(solution)/shard_map/all_to_all | solution.py:200
  216.1 5.6 convert_reduce_fusion.1
  224.1 4.8 convert_reduce_fusion.4
  229.0 5.6 fusion.19
  238.8 3.6 convolution_bitcast_fusion
  242.5 6.1 copy.457
  249.7 5.6 fusion.146
  256.1 5.6 fusion.143
  262.8 4.9 fusion.160
  274.1 6.5 fusion.147
  280.6 6.9 convolution_convert_fusion
  289.7 4.2 all-to-all-start.4
  293.9 5.8 add_convert_fusion
  301.9 11.5 %all-to-all-done.4 = bf16[4,768,128]{2,0,1:T(4,128)(2,1)} async-done(((bf16[4,768,128]{2,0,1:T(4,128)(2,1)}), bf16[4,768,128]{2,0,1:T(4,128)(2,1)}, u32[]{:S(2)}, u32[]{:S(2)}) %all-to-all-start.4) | async-done | bytes 786464 | tf_op jit(solution)/shard_map/all_to_all | solution.py:269
  313.4 4.2 all-to-all-start.3
  326.2 44.4 %all-reduce.8 = (f32[3200]{0:T(1024)}, f32[1536]{0:T(1024)}, f32[768]{0:T(1024)}, f32[2,128]{1,0:T(2,128)}, f32[2,128]{1,0:T(2,128)}, /*index=5*/f32[768]{0:T(10...) all-reduce(f32[3200]{0:T(1024)S(1)} %convert_reduce_fusion, ...), channel_id=1, replica_groups=mesh['ch'=8,'tok'=4] {'ch','tok'}, use_global_device_ids=true, to_apply=%region_33.34 | all-reduce | flops 9856 | bytes 78848 | tf_op jit(solution)/shard_map/psum | solution.py:311
  383.1 5.1 fusion.30
  395.3 3.7 multiply_reduce_fusion.6
  399.1 6.1 all-gather.2
  413.0 11.1 %add_bitcast_fusion = f32[4,96,8,128]{3,2,0,1:T(8,128)} fusion(f32[96,4,8,128]{3,2,1,0:T(8,128)S(1)} %fusion.80, f32[96,128,128,1]{2,0,1,3:T(8,128)} %fusion.28, f32[4,96,8,128]{3,2,0,1:T(8,128)S(1)} %copy-done.11), kind=kOutput, calls=%fused_computation.105 | convolution fusion | flops 604372992 | bytes 11010048 | tf_op jit(solution)/shard_map/transpose(jvp(dts,ndbs->ndbt))/dot_general | solution.py:49
  427.4 4.8 multiply_reduce_fusion.14
  432.3 5.1 bitcast_add_fusion.2
  437.3 6.2 multiply_reduce_fusion
  445.8 10.3 %reduce-scatter.14.cloned.1.call-done = f32[192,768]{1,0:T(8,128)} async-done(((f32[1536,768]{1,0:T(8,128)}), f32[192,768]{1,0:T(8,128)}) %reduce-scatter.14.cloned.1.call-update) | async-done | bytes 589840 | tf_op jit(solution)/shard_map/reduce_scatter | solution.py:294
  456.1 98.7 %reduce-scatter.12.cloned.1.call-done = f32[96,1536]{1,0:T(8,128)} async-done(((f32[768,1536]{1,0:T(8,128)}), f32[96,1536]{1,0:T(8,128)}) %reduce-scatter.12.cloned.1.call-update) | async-done | bytes 589840 | tf_op jit(solution)/shard_map/reduce_scatter | solution.py:293
  554.8 98.7 %reduce-scatter.10.cloned.1.call-done = f32[192,768]{1,0:T(8,128)} async-done(((f32[1536,768]{1,0:T(8,128)}), f32[192,768]{1,0:T(8,128)}) %reduce-scatter.10.cloned.1.call-update) | async-done | bytes 589840 | tf_op jit(solution)/shard_map/reduce_scatter | solution.py:292
  653.5 172.2 %reduce-scatter.8.cloned.1.call-done = f32[96,3200]{1,0:T(8,128)} async-done(((f32[768,3200]{1,0:T(8,128)}), f32[96,3200]{1,0:T(8,128)}) %reduce-scatter.8.cloned.1.call-update) | async-done | bytes 1228816 | tf_op jit(solution)/shard_map/reduce_scatter | solution.py:290
  834.8 5.1 convolution_bitcast_fusion.1
  840.0 7.9 fusion.2
  849.6 5.5 multiply_reduce_fusion.11
  856.3 13.3 %all-reduce.9 = (f32[96,16]{0,1:T(8,128)}, f32[96,16]{0,1:T(8,128)}, f32[96,16]{0,1:T(8,128)}, f32[96,16]{0,1:T(8,128)}, f32[96]{0:T(128)}) all-reduce(f32[96,16]{0,1:T(8,128)S(1)} %get-tuple-element.536, f32[96,16]{0,1:T(8,128)S(1)} %get-tuple-element.535, ...), channel_id=1, replica_groups=mesh['ch'=8,'tok'=4] {'tok'}, use_global_device_ids=true, to_apply=%region_23.24 | all-reduce | flops 6240 | bytes 49920 | tf_op jit(solution)/shard_map/psum | solution.py:296
  869.6 38.3 %all-reduce.13.cloned.1.call-done = (f32[96,3200]{1,0:T(8,128)}, f32[96,1536]{0,1:T(8,128)}, f32[192,768]{1,0:T(8,128)}, f32[96,1536]{1,0:T(8,128)}, f32[192,768]{1,0:T(8,128)}) async-done(((f32[96,3200]{1,0:T(8,128)}, f32[96,1536]{0,1:T(8,128)}, f32[192,768]{1,0:T(8,128)}, f32[96,1536]{1,0:T(8,128)}, f32[192,768]{1,0:T(8,128)}), (f32[96,3200]{1,0:T(8,128)}, f32[96,1536]{0,1:T(8,128)}, ...) | async-done | bytes 3588112 | tf_op jit(solution)/shard_map/psum | solution.py:296
  (459 shorter events, 164.3 us)
Async XLA Ops:
  7.2 135.1 %copy-start = (bf16[1536,768]{1,0:T(8,128)(2,1)S(1)}, bf16[1536,768]{1,0:T(8,128)(2,1)}, u32[]{:S(2)}) copy-start(bf16[1536,768]{1,0:T(8,128)(2,1)} %param.38) | copy-start | bytes 7077892
  7.2 10.4 %copy-start.85 = (f32[96,16]{0,1:T(8,128)S(1)}, f32[96,16]{0,1:T(8,128)}, u32[]{:S(2)}) copy-start(f32[96,16]{0,1:T(8,128)} %param.32) | copy-start | bytes 18436
  7.2 10.4 %copy-start.100 = (f32[96,16]{0,1:T(8,128)S(1)}, f32[96,16]{0,1:T(8,128)}, u32[]{:S(2)}) copy-start(f32[96,16]{0,1:T(8,128)} %param.31) | copy-start | bytes 18436
  7.2 10.4 %copy-start.104 = (f32[96,16]{0,1:T(8,128)S(1)}, f32[96,16]{0,1:T(8,128)}, u32[]{:S(2)}) copy-start(f32[96,16]{0,1:T(8,128)} %param.30) | copy-start | bytes 18436
  7.2 10.4 %copy-start.102 = (f32[96,16]{0,1:T(8,128)S(1)}, f32[96,16]{0,1:T(8,128)}, u32[]{:S(2)}) copy-start(f32[96,16]{0,1:T(8,128)} %param.29) | copy-start | bytes 18436
  9.8 81.8 %all-to-all-start.1 = ((bf16[4,96,1024]{1,0,2:T(4,128)(2,1)}), bf16[4,96,1024]{1,0,2:T(4,128)(2,1)}, u32[]{:S(2)}, u32[]{:S(2)}) async-start(bf16[4,96,1024]{1,0,2:T(4,128)(2,1)} %copy.385), calls=%async_computation.1 | async-start | bytes 2097152 | tf_op jit(solution)/shard_map/all_to_all | solution.py:130
  17.0 13.5 %copy-start.15 = (bf16[4,96,1024]{2,1,0:T(8,128)(2,1)S(1)}, bf16[4,96,1024]{2,1,0:T(8,128)(2,1)}, u32[]{:S(2)}) copy-start(bf16[4,96,1024]{2,1,0:T(8,128)(2,1)} %param.26) | copy-start | bytes 2359300
  18.3 12.1 %copy-start.87 = (f32[96,16]{0,1:T(8,128)}, f32[96,16]{0,1:T(8,128)S(1)}, u32[]{:S(2)}) copy-start(f32[96,16]{0,1:T(8,128)S(1)} %get-tuple-element.512) | copy-start | bytes 18436
  18.4 17.2 %copy-start.55 = (f32[96,16]{1,0:T(8,128)}, f32[96,16]{1,0:T(8,128)S(1)}, u32[]{:S(2)}) copy-start(f32[96,16]{1,0:T(8,128)S(1)} %copy.363) | copy-start | bytes 18436
  19.1 16.5 %copy-start.52 = (f32[96,16]{1,0:T(8,128)}, f32[96,16]{1,0:T(8,128)S(1)}, u32[]{:S(2)}) copy-start(f32[96,16]{1,0:T(8,128)S(1)} %copy.366) | copy-start | bytes 18436
  50.0 18.3 %copy-start.32 = (f32[96,8,16]{2,1,0:T(8,128)}, f32[96,8,16]{2,1,0:T(8,128)S(1)}, u32[]{:S(2)}) copy-start(f32[96,8,16]{2,1,0:T(8,128)S(1)} %multiply_exponential_fusion.4) | copy-start | bytes 147460
  91.6 9.2 %copy-start.120 = (f32[2,128]{1,0:T(2,128)S(1)}, f32[2,128]{1,0:T(2,128)}, u32[]{:S(2)}) copy-start(f32[2,128]{1,0:T(2,128)} %param.40) | copy-start | bytes 3076
  91.6 9.2 %copy-start.126 = (f32[2,128]{1,0:T(2,128)S(1)}, f32[2,128]{1,0:T(2,128)}, u32[]{:S(2)}) copy-start(f32[2,128]{1,0:T(2,128)} %param.41) | copy-start | bytes 3076
  91.6 9.2 %copy-start.127 = (s32[4]{0:T(128)S(1)}, s32[4]{0:T(128)}, u32[]{:S(2)}) copy-start(s32[4]{0:T(128)} %param.28) | copy-start | bytes 52
  91.6 32.5 %all-to-all-start = ((bf16[4,96,1024]{1,0,2:T(4,128)(2,1)}), bf16[4,96,1024]{1,0,2:T(4,128)(2,1)}, u32[]{:S(2)}, u32[]{:S(2)}) async-start(bf16[4,96,1024]{1,0,2:T(4,128)(2,1)} %copy.381), calls=%async_computation | async-start | bytes 2097152 | tf_op jit(solution)/shard_map/all_to_all | solution.py:131
  97.7 345.9 %reduce-scatter.16.cloned.1.call-start = ((), (), s32[]{:S(2)}) async-start(), calls=%async_computation.14 | async-start | bytes 5308416
  134.6 7.0 copy-start.31
  151.0 8.0 collective-permute-start
  152.5 9.2 collective-permute-start.1
  152.5 10.6 %collective-permute-start.2 = (bf16[4,96,128]{1,0,2:T(4,128)(2,1)S(1)}, bf16[4,96,128]{1,0,2:T(4,128)(2,1)S(1)}, u32[]{:S(2)}, u32[]{:S(2)}) collective-permute-start(bf16[4,96,128]{1,0,2:T(4,128)(2,1)S(1)} %bitcast.352), channel_id=1, source_target_pairs={{0,12},{4,8},{8,4},{12,0},{16,28},{20,24},{24,20},{28,16},{1,13},{... | collective-permute-start | bytes 294920 | tf_op jit(solution)/shard_map/ppermute | solution.py:193
  154.5 18.5 %collective-permute-start.3 = (bf16[4,96,128]{1,0,2:T(4,128)(2,1)S(1)}, bf16[4,96,128]{1,0,2:T(4,128)(2,1)S(1)}, u32[]{:S(2)}, u32[]{:S(2)}) collective-permute-start(bf16[4,96,128]{1,0,2:T(4,128)(2,1)S(1)} %bitcast.351), channel_id=1, source_target_pairs={{0,16},{4,20},{8,24},{12,28},{16,0},{20,4},{24,8},{28,12},{1,17},{... | collective-permute-start | bytes 294920 | tf_op jit(solution)/shard_map/ppermute | solution.py:193
  155.0 21.7 %collective-permute-start.4 = (bf16[4,96,128]{1,0,2:T(4,128)(2,1)S(1)}, bf16[4,96,128]{1,0,2:T(4,128)(2,1)S(1)}, u32[]{:S(2)}, u32[]{:S(2)}) collective-permute-start(bf16[4,96,128]{1,0,2:T(4,128)(2,1)S(1)} %bitcast.350), channel_id=1, source_target_pairs={{0,20},{4,16},{8,28},{12,24},{16,4},{20,0},{24,12},{28,8},{1,21},{... | collective-permute-start | bytes 294920 | tf_op jit(solution)/shard_map/ppermute | solution.py:193
  158.3 18.6 %copy-start.30 = (bf16[4,96,1024]{1,0,2:T(4,128)(2,1)S(1)}, bf16[4,96,1024]{1,0,2:T(4,128)(2,1)}, u32[]{:S(2)}) copy-start(bf16[4,96,1024]{1,0,2:T(4,128)(2,1)} %copy.398) | copy-start | bytes 2359300
  158.3 18.6 %copy-start.68 = (pred[4,1024]{0,1:T(8,128)(4,1)S(1)}, pred[4,1024]{0,1:T(8,128)(4,1)}, u32[]{:S(2)}) copy-start(pred[4,1024]{0,1:T(8,128)(4,1)} %broadcast_compare_fusion) | copy-start | bytes 12292
  159.0 17.8 %collective-permute-start.5 = (bf16[4,96,128]{1,0,2:T(4,128)(2,1)S(1)}, bf16[4,96,128]{1,0,2:T(4,128)(2,1)S(1)}, u32[]{:S(2)}, u32[]{:S(2)}) collective-permute-start(bf16[4,96,128]{1,0,2:T(4,128)(2,1)S(1)} %bitcast.349), channel_id=1, source_target_pairs={{0,24},{4,28},{8,16},{12,20},{16,8},{20,12},{24,0},{28,4},{1,25},{... | collective-permute-start | bytes 294920 | tf_op jit(solution)/shard_map/ppermute | solution.py:193
  161.7 15.2 %collective-permute-start.6 = (bf16[4,96,128]{1,0,2:T(4,128)(2,1)S(1)}, bf16[4,96,128]{1,0,2:T(4,128)(2,1)S(1)}, u32[]{:S(2)}, u32[]{:S(2)}) collective-permute-start(bf16[4,96,128]{1,0,2:T(4,128)(2,1)S(1)} %bitcast.348), channel_id=1, source_target_pairs={{0,28},{4,24},{8,20},{12,16},{16,12},{20,8},{24,4},{28,0},{1,29},{... | collective-permute-start | bytes 294920 | tf_op jit(solution)/shard_map/ppermute | solution.py:193
  248.6 207.5 %reduce-scatter.14.cloned.1.call-start = ((), (), s32[]{:S(2)}) async-start(), calls=%async_computation.13 | async-start | bytes 5308416 | tf_op jit(solution)/shard_map/reduce_scatter | solution.py:294
  255.4 299.4 %reduce-scatter.12.cloned.1.call-start = ((), (), s32[]{:S(2)}) async-start(), calls=%async_computation.12 | async-start | bytes 5308416 | tf_op jit(solution)/shard_map/reduce_scatter | solution.py:293
  261.7 391.8 %reduce-scatter.10.cloned.1.call-start = ((), (), s32[]{:S(2)}) async-start(), calls=%async_computation.11 | async-start | bytes 5308416 | tf_op jit(solution)/shard_map/reduce_scatter | solution.py:292
  267.8 558.0 %reduce-scatter.8.cloned.1.call-start = ((), (), s32[]{:S(2)}) async-start(), calls=%async_computation.10 | async-start | bytes 11059200 | tf_op jit(solution)/shard_map/reduce_scatter | solution.py:290
  289.7 23.7 %all-to-all-start.4 = ((bf16[4,768,128]{2,0,1:T(4,128)(2,1)}), bf16[4,768,128]{2,0,1:T(4,128)(2,1)}, u32[]{:S(2)}, u32[]{:S(2)}) async-start(bf16[4,768,128]{2,0,1:T(4,128)(2,1)} %bitcast.330), calls=%async_computation.4 | async-start | bytes 1572864 | tf_op jit(solution)/shard_map/all_to_all | solution.py:269
  313.4 63.4 %all-to-all-start.3 = ((bf16[4,768,128]{2,0,1:T(4,128)(2,1)}), bf16[4,768,128]{2,0,1:T(4,128)(2,1)}, u32[]{:S(2)}, u32[]{:S(2)}) async-start(bf16[4,768,128]{2,0,1:T(4,128)(2,1)} %bitcast.53), calls=%async_computation.3 | async-start | bytes 1572864 | tf_op jit(solution)/shard_map/all_to_all | solution.py:262
  317.6 590.3 %all-reduce.13.cloned.1.call-start = ((), (), s32[]{:S(2)}) async-start(), calls=%async_computation.15 | async-start | bytes 7569408 | tf_op jit(solution)/shard_map/psum | solution.py:296
  395.3 9.9 %copy-start.41 = (f32[4,96,16]{1,2,0:T(8,128)S(1)}, f32[4,96,16]{1,2,0:T(8,128)}, u32[]{:S(2)}) copy-start(f32[4,96,16]{1,2,0:T(8,128)} %custom-call.1) | copy-start | bytes 73732
  839.9 8.0 copy-start.58
  839.9 9.5 %copy-start.40 = (f32[4,96,16]{2,0,1:T(4,128)S(1)}, f32[4,96,16]{2,0,1:T(4,128)}, u32[]{:S(2)}) copy-start(f32[4,96,16]{2,0,1:T(4,128)} %copy.377) | copy-start | bytes 73732
  840.0 9.5 %copy-start.62 = (f32[96,16,128]{2,1,0:T(8,128)S(1)}, f32[96,16,128]{2,1,0:T(8,128)}, u32[]{:S(2)}) copy-start(f32[96,16,128]{2,1,0:T(8,128)} %rev.11) | copy-start | bytes 2359300
  840.0 9.5 %copy-start.70 = (f32[96,16]{1,0:T(8,128)S(1)}, f32[96,16]{1,0:T(8,128)}, u32[]{:S(2)}) copy-start(f32[96,16]{1,0:T(8,128)} %copy.378) | copy-start | bytes 18436
  840.0 9.5 %copy-start.72 = (f32[96,16]{1,0:T(8,128)S(1)}, f32[96,16]{1,0:T(8,128)}, u32[]{:S(2)}) copy-start(f32[96,16]{1,0:T(8,128)} %copy.379) | copy-start | bytes 18436
  840.0 9.5 %copy-start.91 = (f32[96,16]{1,0:T(8,128)S(1)}, f32[96,16]{1,0:T(8,128)}, u32[]{:S(2)}) copy-start(f32[96,16]{1,0:T(8,128)} %copy.421) | copy-start | bytes 18436
  849.5 6.6 copy-start.84
  849.5 6.6 copy-start.86
  849.5 6.6 copy-start.88
  849.5 6.6 copy-start.95
  849.5 6.6 copy-start.96
  849.5 6.6 copy-start.97
  849.6 6.6 copy-start.98
  849.6 6.7 copy-start.123
  (110 other events, 329.8 us)
Sparse Core Ops, SparseCore 0:
  248.7 109.4 reduce-scatter.15
  361.8 94.2 reduce-scatter.13
  459.8 95.0 reduce-scatter.11
  558.3 95.1 reduce-scatter.9
  657.0 168.6 reduce-scatter.7
  828.3 79.5 all-reduce.12
